TPU v7x, 32 devices: a whole 2x2x4 slice. The times are simulated.
32 devices in a mesh: groups: 2 (over x), slab: 8 (over z, y), sub: 2 (over core).
Axes of the slice: x: 2, y: 2, z: 4, core: 2. Of those that a mesh axis runs over, the one named last changes fastest.
Arguments:
- features: float32 [128, 64, 512], P(('groups', 'slab'), 'sub'), parts along dimension 0, may hold values from -6 to 6
- block_count: int32 [16], P(('groups', 'slab')), parts along dimension 0, may hold values from 4 to 8, as said below
- neighbours: int32 [128, 27], P(('groups', 'slab')), parts along dimension 0, may hold values from 0 to 24, as said below
- conv_weight: float32 [27, 64, 64], P(None, 'sub'), may hold values from -0.15625 to 0.15625
- lift_weight: float32 [128, 64], replicated, may hold values from -0.75 to 0.75
- drop_weight: float32 [64, 128], P('sub'), may hold values from -0.5 to 0.5
- cotangent: float32 [128, 64, 512], P(('groups', 'slab'), 'sub'), parts along dimension 0, may hold values from -6 to 6
Outputs:
- output: float32 [128, 64, 512], P(('groups', 'slab'), 'sub'), parts along dimension 0
- feature_grad: float32 [128, 64, 512], P(('groups', 'slab'), 'sub'), parts along dimension 0
- weight_grad: float32 [27, 128, 64], P(None, ('groups', 'sub')), parts along dimension 1
There are 2 independent parts, one for each index of `groups`. A program takes and returns all parts, laid end to end along the dimension named above; an argument that names none is the same for every part. Nothing has to cross between parts.
Inputs may be any that keep to these rules, and one draw needn't show every extreme that they name: `block_count`: each slab has between 4 and 8 live slots, the live ones first; some slab has all 8 live. `neighbours`: entries are 3 * 8 (no neighbour) or a slot of slab s-1 (0 .. 7), s (8 .. 15) or s+1 (16 .. 23) of the table; the centre offset 13 is the block itself. Slabs at the ends name no slab beyond them.
All inputs are finite; a program needn't handle non-finite values.
Results may differ from a plain program's by a relative error of at most 0.00008.
Values sent between devices are 32-bit elements; how exact they have to be, the bound alone decides.
A program may use at most 128 MiB of HBM per device.

v0:
```python
import jax
import jax.numpy as jnp
from jax import lax
from jax.sharding import PartitionSpec as P

HIGH = lax.Precision.HIGHEST


def extended(array, sides, width):
    for axis, dim in sides:
        size, length = (lax.axis_size(axis), array.shape[dim])
        up = [(i, (i + 1) % size) for i in range(size - 1)]
        down = [(j, i) for i, j in up]
        last = lax.slice_in_dim(array, length - width, length, axis=dim)
        leading = lax.slice_in_dim(array, 0, width, axis=dim)
        before = lax.ppermute(last, axis, up)
        after = lax.ppermute(leading, axis, down)
        array = jnp.concatenate([before, array, after], axis=dim)
    return array


def from_behind(array, axis, by):
    length = lax.axis_size(axis)
    pairs = [(i, i + by) for i in range(length) if 0 <= i + by < length]
    return lax.ppermute(array, axis, pairs)


def assemble(near):
    first = jnp.concatenate([near[0][..., 7:8, :, :], near[1], near[2][..., 0:1, :, :]], axis=-3)
    second = jnp.concatenate([first[0][..., 7:8, :], first[1], first[2][..., 0:1, :]], axis=-2)
    return jnp.concatenate([second[0][..., 7:8], second[1], second[2][..., 0:1]], axis=-1)


def conv_blocks(table, rows, weight):
    chans = table.shape[1]

    def single(row):
        near = table[row].reshape(3, 3, 3, chans, 8, 8, 8)
        patch = assemble(near)
        cols = jnp.stack(
            [
                patch[:, a : a + 8, b : b + 8, c : c + 8].reshape(chans, 512)
                for a in range(3)
                for b in range(3)
                for c in range(3)
            ]
        )
        return jnp.einsum("koi,kiv->ov", weight, cols, precision=HIGH)

    return lax.map(jax.checkpoint(single), rows)


def pool_blocks(fine):
    count, chans, _ = fine.shape
    view = fine.reshape(count // 8, 2, 2, 2, chans, 4, 2, 4, 2, 4, 2).mean(axis=(6, 8, 10))
    return view.transpose(0, 4, 1, 5, 2, 6, 3, 7).reshape(count // 8, chans, 512)


def spread_blocks(coarse):
    count, chans, _ = coarse.shape
    view = coarse.reshape(count, chans, 2, 4, 2, 4, 2, 4).transpose(0, 2, 4, 6, 1, 3, 5, 7)
    view = jnp.broadcast_to(
        view[..., :, None, :, None, :, None], (count, 2, 2, 2, chans, 4, 2, 4, 2, 4, 2)
    )
    return view.reshape(count * 8, chans, 512)


def shards(features, block_count, neighbours, conv_weight, lift_weight, drop_weight, cotangent):
    blocks = features.shape[0]
    mine = features.shape[1]
    first = lax.axis_index("sub") * mine
    narrow = extended(features, (("slab", 0),), blocks)
    padded = lax.all_gather(narrow, "sub", axis=1, tiled=True)

    def local_conv(table_part, weight):
        table = jnp.concatenate(
            [table_part, jnp.zeros((1,) + table_part.shape[1:], table_part.dtype)], axis=0
        )
        return conv_blocks(table, neighbours, weight)

    pre, pull = jax.vjp(local_conv, padded, conv_weight)
    live = (lax.iota(jnp.int32, blocks) < block_count[0]).astype(jnp.float32)[:, None, None]
    sig = jax.nn.sigmoid(pre)
    hidden = pre * sig
    pooled_own = pool_blocks(hidden * live)
    lift_own = lax.dynamic_slice_in_dim(lift_weight, first, mine, 1)
    pooled = lax.all_gather(pooled_own, "sub", axis=1, tiled=True)
    lifted_pre = jnp.einsum("hc,ncv->nhv", lift_weight, pooled, precision=HIGH)
    lift_sig = jax.nn.sigmoid(lifted_pre)
    lifted = lifted_pre * lift_sig
    coarse = jnp.einsum("ch,nhv->ncv", drop_weight, lifted, precision=HIGH)
    output = live * (hidden + spread_blocks(coarse))
    out_grad = live * cotangent
    coarse_grad = pool_blocks(out_grad) * 8.0
    lifted_grad = lax.psum(
        jnp.einsum("ch,ncv->nhv", drop_weight, coarse_grad, precision=HIGH), "sub"
    )
    lifted_pre_grad = lifted_grad * lift_sig * (1.0 + lifted_pre * (1.0 - lift_sig))
    pooled_grad = jnp.einsum("hc,nhv->ncv", lift_own, lifted_pre_grad, precision=HIGH)
    hidden_grad = out_grad + live * spread_blocks(pooled_grad) * 0.125
    pre_grad = hidden_grad * sig * (1.0 + pre * (1.0 - sig))
    scale = 1.0 / jnp.sqrt(jnp.float32(512 * blocks * lax.axis_size("slab")))
    table_grad, weight_part = pull(pre_grad)
    table_mine = lax.psum_scatter(table_grad, "sub", scatter_dimension=1, tiled=True)
    lower = table_mine[:blocks]
    middle = table_mine[blocks : 2 * blocks]
    upper = table_mine[2 * blocks :]
    feature_grad = middle + from_behind(lower, "slab", -1) + from_behind(upper, "slab", 1)
    weight_grad = lax.psum(weight_part, "slab") * scale
    return (output, feature_grad, weight_grad)


def solution(mesh):
    return jax.shard_map(
        shards,
        mesh=mesh,
        in_specs=(
            P(("groups", "slab"), "sub", None),
            P(("groups", "slab")),
            P(("groups", "slab"), None),
            P(None, "sub", None),
            P(),
            P("sub", None),
            P(("groups", "slab"), "sub", None),
        ),
        out_specs=(
            P(("groups", "slab"), "sub", None),
            P(("groups", "slab"), "sub", None),
            P(None, ("groups", "sub"), None),
        ),
        check_vma=False,
    )
```

profile of v0, /device:TPU:0, one launch (start us, length us, event | category | flops | bytes accessed | tf_op | source)
XLA Modules:
  0.0 1874.4 jit_solution(15311587361316387911)
XLA Ops:
  14.2 10.2 collective-permute-done.1
  24.4 11.5 collective-permute-done
  40.9 10.7 all-gather.2.cloned.1.call-done
  54.0 478.9 %while.27 = (s32[]{:T(128)}, f32[8,32,512]{2,1,0:T(8,128)}, s32[8,27]{1,0:T(8,128)S(1)}, f32[25,64,512]{2,1,0:T(8,128)S(1)}, f32[27,32,64]{2,1,0:T(8,128)}, /*index=5*/s32[]{:T(128)}) while((s32[]{:T(128)}, f32[8,32,512]{2,1,0:T(8,128)}, s32[8,27]{1,0:T(8,128)S(1)}, f32[25,64,512]{2,1,0:T(8,128)S(1)}, f32[27,32,64]{2,1,0:T(8,128)}, ...), condition=%wide.region_1.2_spmd, body=%wide.region_0.1_spmd.sunk | while | flops 341374048 | bytes 92386016 | solution.py:50
  559.6 15.2 all-reduce.46.cloned.1.call-done
  588.9 1169.1 %while.28 = (s32[]{:T(128)}, f32[25,64,512]{2,1,0:T(8,128)}, f32[27,32,64]{2,1,0:T(8,128)}, s32[8,27]{1,0:T(8,128)S(1)}, f32[8,32,512]{2,1,0:T(8,128)}, /*index=...) while((s32[]{:T(128)}, f32[25,64,512]{2,1,0:T(8,128)}, ...), condition=%wide.region_7.8_spmd.clone, body=%wide.region_5.7_spmd.clone.sunk | while | flops 686794880 | bytes 157496352 | solution.py:50
  669.5 6.3 copy.452
  675.8 9.2 scatter_fusion
  739.8 7.1 fusion.105
  813.7 6.3 copy.452
  820.0 9.4 scatter_fusion
  884.2 7.2 fusion.105
  958.2 6.3 copy.452
  964.5 9.3 scatter_fusion
  1028.6 7.2 fusion.105
  1102.6 6.3 copy.452
  1108.9 9.3 scatter_fusion
  1173.0 7.2 fusion.105
  1247.0 6.3 copy.452
  1253.3 9.2 scatter_fusion
  1317.3 7.2 fusion.105
  1391.3 6.3 copy.452
  1397.6 9.4 scatter_fusion
  1461.9 7.2 fusion.105
  1535.9 6.3 copy.452
  1542.1 9.2 scatter_fusion
  1606.2 7.2 fusion.105
  1680.2 6.3 copy.452
  1686.5 9.5 scatter_fusion
  1750.8 7.2 fusion.105
  1762.1 13.4 reduce-scatter.2.cloned.1.call-done
  1783.9 79.8 %all-reduce.48.cloned.1.call-done = f32[27,32,64]{2,1,0:T(8,128)} async-done(((f32[27,32,64]{2,1,0:T(8,128)}), f32[27,32,64]{2,1,0:T(8,128)}) %all-reduce.48.cloned.1.call-update) | async-done | bytes 221200 | tf_op jit(solution)/shard_map/psum | solution.py:109
  (1841 shorter events, 1516.3 us)
Async XLA Ops:
  7.2 548.1 %copy-start = (f32[128,64]{0,1:T(8,128)S(1)}, f32[128,64]{0,1:T(8,128)}, u32[]{:S(2)}) copy-start(f32[128,64]{0,1:T(8,128)} %param.15) | copy-start | bytes 98308
  7.2 31.2 %copy-start.18 = (f32[8,32,512]{2,1,0:T(8,128)S(1)}, f32[8,32,512]{2,1,0:T(8,128)}, u32[]{:S(2)}) copy-start(f32[8,32,512]{2,1,0:T(8,128)} %param.17) | copy-start | bytes 1572868
  7.2 44.4 %all-gather.2.cloned.1.call-start = ((), (), s32[]{:S(2)}) async-start(), calls=%async_computation.1 | async-start | bytes 4718592 | tf_op jit(solution)/shard_map/all_gather | solution.py:73
  7.2 17.1 collective-permute-start.1
  8.7 27.2 %collective-permute-start = (f32[8,32,512]{2,1,0:T(8,128)}, f32[8,32,512]{2,1,0:T(8,128)S(1)}, u32[]{:S(2)}, u32[]{:S(2)}) collective-permute-start(f32[8,32,512]{2,1,0:T(8,128)} %param.11), channel_id=1, source_target_pairs={{0,2},{2,4},{4,6},{6,8},{8,10},{10,12},{12,14},{1,3},{3,5},{5,7},{... | collective-permute-start | bytes 1572872 | tf_op jit(solution)/shard_map/ppermute | solution.py:16
  38.3 536.5 %all-reduce.46.cloned.1.call-start = ((), (), s32[]{:S(2)}) async-start(), calls=%async_computation.2 | async-start | bytes 524288 | tf_op jit(solution)/shard_map/psum | solution.py:95
  200.7 14.3 copy-start.9
  260.6 14.3 copy-start.9
  320.5 14.3 copy-start.9
  380.3 14.3 copy-start.9
  555.2 1220.3 %reduce-scatter.2.cloned.1.call-start = ((), (), s32[]{:S(2)}) async-start(), calls=%async_computation.3 | async-start | bytes 4718592 | tf_op jit(solution)/shard_map/reduce_scatter | solution.py:104
  602.7 82.3 %copy-start.4 = (f32[25,64,512]{2,1,0:T(8,128)}, f32[25,64,512]{2,1,0:T(8,128)S(1)}, u32[]{:S(2)}) copy-start(f32[25,64,512]{2,1,0:T(8,128)S(1)} %get-tuple-element.633) | copy-start | bytes 9830404 | tf_op jit(solution)/shard_map/transpose(jvp())/while
  708.7 14.5 copy-start.11
  747.0 82.5 %copy-start.4 = (f32[25,64,512]{2,1,0:T(8,128)}, f32[25,64,512]{2,1,0:T(8,128)S(1)}, u32[]{:S(2)}) copy-start(f32[25,64,512]{2,1,0:T(8,128)S(1)} %get-tuple-element.633) | copy-start | bytes 9830404 | tf_op jit(solution)/shard_map/transpose(jvp())/while
  853.1 14.5 copy-start.11
  891.4 82.4 %copy-start.4 = (f32[25,64,512]{2,1,0:T(8,128)}, f32[25,64,512]{2,1,0:T(8,128)S(1)}, u32[]{:S(2)}) copy-start(f32[25,64,512]{2,1,0:T(8,128)S(1)} %get-tuple-element.633) | copy-start | bytes 9830404 | tf_op jit(solution)/shard_map/transpose(jvp())/while
  997.5 14.5 copy-start.11
  1035.8 82.3 %copy-start.4 = (f32[25,64,512]{2,1,0:T(8,128)}, f32[25,64,512]{2,1,0:T(8,128)S(1)}, u32[]{:S(2)}) copy-start(f32[25,64,512]{2,1,0:T(8,128)S(1)} %get-tuple-element.633) | copy-start | bytes 9830404 | tf_op jit(solution)/shard_map/transpose(jvp())/while
  1141.9 14.5 copy-start.11
  1180.2 82.3 %copy-start.4 = (f32[25,64,512]{2,1,0:T(8,128)}, f32[25,64,512]{2,1,0:T(8,128)S(1)}, u32[]{:S(2)}) copy-start(f32[25,64,512]{2,1,0:T(8,128)S(1)} %get-tuple-element.633) | copy-start | bytes 9830404 | tf_op jit(solution)/shard_map/transpose(jvp())/while
  1286.2 14.5 copy-start.11
  1324.5 82.5 %copy-start.4 = (f32[25,64,512]{2,1,0:T(8,128)}, f32[25,64,512]{2,1,0:T(8,128)S(1)}, u32[]{:S(2)}) copy-start(f32[25,64,512]{2,1,0:T(8,128)S(1)} %get-tuple-element.633) | copy-start | bytes 9830404 | tf_op jit(solution)/shard_map/transpose(jvp())/while
  1430.8 14.5 copy-start.11
  1469.1 82.3 %copy-start.4 = (f32[25,64,512]{2,1,0:T(8,128)}, f32[25,64,512]{2,1,0:T(8,128)S(1)}, u32[]{:S(2)}) copy-start(f32[25,64,512]{2,1,0:T(8,128)S(1)} %get-tuple-element.633) | copy-start | bytes 9830404 | tf_op jit(solution)/shard_map/transpose(jvp())/while
  1575.1 14.5 copy-start.11
  1613.4 82.6 %copy-start.4 = (f32[25,64,512]{2,1,0:T(8,128)}, f32[25,64,512]{2,1,0:T(8,128)S(1)}, u32[]{:S(2)}) copy-start(f32[25,64,512]{2,1,0:T(8,128)S(1)} %get-tuple-element.633) | copy-start | bytes 9830404 | tf_op jit(solution)/shard_map/transpose(jvp())/while
  1719.7 14.5 copy-start.11
  1762.0 20.5 %copy-start.17 = (f32[8,32,512]{1,2,0:T(8,128)S(1)}, f32[8,32,512]{1,2,0:T(8,128)}, u32[]{:S(2)}) copy-start(f32[8,32,512]{1,2,0:T(8,128)} %get-tuple-element.369) | copy-start | bytes 1572868
  1762.1 101.6 %all-reduce.48.cloned.1.call-start = ((), (), s32[]{:S(2)}) async-start(), calls=%async_computation.4 | async-start | bytes 884736 | tf_op jit(solution)/shard_map/psum | solution.py:109
  1775.5 92.2 %copy-start.1 = (f32[128,64]{0,1:T(8,128)S(1)}, f32[128,64]{0,1:T(8,128)}, u32[]{:S(2)}) copy-start(f32[128,64]{0,1:T(8,128)} %param.15) | copy-start | bytes 98308
  1777.6 87.9 %collective-permute-start.3 = (f32[8,32,512]{2,1,0:T(8,128)}, f32[8,32,512]{2,1,0:T(8,128)S(1)}, u32[]{:S(2)}, u32[]{:S(2)}) collective-permute-start(f32[8,32,512]{2,1,0:T(8,128)} %get-tuple-element.371), channel_id=1, source_target_pairs={{0,2},{2,4},{4,6},{6,8},{8,10},{10,12},{12,14},{1,3},{3,5},{5,7},{... | collective-permute-start | bytes 1572872 | tf_op jit(solution)/shard_map/ppermute | solution.py:25
  1781.2 84.3 %collective-permute-start.2 = (f32[8,32,512]{2,1,0:T(8,128)S(1)}, f32[8,32,512]{2,1,0:T(8,128)}, u32[]{:S(2)}, u32[]{:S(2)}) collective-permute-start(f32[8,32,512]{2,1,0:T(8,128)S(1)} %get-tuple-element.370), channel_id=1, source_target_pairs={{2,0},{4,2},{6,4},{8,6},{10,8},{12,10},{14,12},{3,1},{5,3},{7,5},{... | collective-permute-start | bytes 1572872 | tf_op jit(solution)/shard_map/ppermute | solution.py:25
  (89 other events, 799.2 us)
Sparse Core Ops, SparseCore 0:
  38.4 13.2 all-gather.1
  555.3 19.4 all-reduce.45
  1762.2 13.2 reduce-scatter.1
  1782.7 80.9 all-reduce.47
where the time goes:
time: 1890 us; the launch traced here: 1870 us
  local copies, waits for them, and re-layouts  1300 us (69%)
  other arithmetic  247 us (13%)
  waiting for transfers between devices  141 us (7%)
  matrix products  135 us (7%)
  loops' own time  20 us (1%)
    another operation x248, local copies, waits for them, and re-layouts, single(): jnp.stack([patch[:, a:a + 8, b:b + 8, c:c + 8].reshape(chans, 512) for a...  410 us
    while x624, local copies, waits for them, and re-layouts  288 us
    reshape x432, local copies, waits for them, and re-layouts, single(): jnp.stack([patch[:, a:a + 8, b:b + 8, c:c + 8].reshape(chans, 512) for a...  228 us
    dot_general x24, matrix products, single(): return jnp.einsum('koi,kiv->ov', weight, cols, precision=HIGH)  131 us
    slice x48, local copies, waits for them, and re-layouts, assemble(): near[0][..., 7:8, :, :]  106 us
    psum x1, waiting for transfers between devices, shards(): weight_grad = lax.psum(weight_part, 'slab') * scale  79.8 us
    scatter-add x8, other arithmetic, single(): near = table[row].reshape(3, 3, 3, chans, 8, 8, 8)  74.5 us
    slice x32, local copies, waits for them, and re-layouts, assemble(): near[2][..., 0:1, :, :]  63 us
  transfers between devices with their start and end apart: 8, of which 6 were waited for; matrix products, arithmetic and copies ran while one was open for 0% of the time, Pallas kernels for 0%

commit v1 on v0

v1 whole, which is shorter than its diff:
```python
import functools

import jax
import jax.numpy as jnp
from jax import lax
from jax.experimental import pallas as pl
from jax.experimental.pallas import tpu as pltpu
from jax.sharding import PartitionSpec as P

HIGH = lax.Precision.HIGHEST
F32 = jnp.float32
BF16 = jnp.bfloat16
K = 27
VOX = 512
LANES = 128
CH = 16
PIECES = VOX // LANES


def split(x):
    hi = x.astype(BF16)
    lo = (x - hi.astype(F32)).astype(BF16)
    return hi, lo


def dot(a, b):
    return jnp.dot(a, b, preferred_element_type=F32)


def dot_nt(a, b):
    return lax.dot_general(a, b, (((1,), (1,)), ((), ())), preferred_element_type=F32)


def rolled(x, by):
    return pltpu.roll(x, by % LANES, axis=1)


def gather_patch(nb_ref, block, table, rows, masks, store):
    half, y0, y7, z0, z7 = masks

    def near(ox, oy, oz, p):
        slot = nb_ref[block, 9 * ox + 3 * oy + oz]
        return table[slot, rows, p * LANES : (p + 1) * LANES]

    def sides(lo, mid, hi, first, last, step):
        before = jnp.where(first, rolled(lo, -7 * step), rolled(mid, step))
        after = jnp.where(last, rolled(hi, 7 * step), rolled(mid, -step))
        return before, mid, after

    for a in range(3):
        for p in range(PIECES):
            plane = []
            for oy in range(3):
                line = []
                for oz in range(3):
                    here = near(1, oy, oz, p)
                    if a == 0:
                        other = near(1, oy, oz, p - 1) if p > 0 else near(0, oy, oz, PIECES - 1)
                        here = rolled(jnp.where(half, here, other), 64)
                    elif a == 2:
                        other = near(1, oy, oz, p + 1) if p < PIECES - 1 else near(2, oy, oz, 0)
                        here = rolled(jnp.where(half, other, here), 64)
                    line.append(here)
                plane.append(line)
            by_z = [sides(plane[0][oz], plane[1][oz], plane[2][oz], y0, y7, 8) for oz in range(3)]
            for b in range(3):
                cells = sides(by_z[0][b], by_z[1][b], by_z[2][b], z0, z7, 1)
                for c in range(3):
                    store(9 * a + 3 * b + c, p, cells[c])


def scatter_patch(nb_ref, block, grads, parts, table_grad, rows, masks, load):
    half, y0, y7, z0, z7 = masks

    def sides(before, mid, after, first, last, step):
        zero = jnp.zeros_like(mid)
        lo = jnp.where(last, rolled(before, 7 * step), zero)
        hi = jnp.where(first, rolled(after, -7 * step), zero)
        mid = mid + jnp.where(last, zero, rolled(before, -step))
        mid = mid + jnp.where(first, zero, rolled(after, step))
        return lo, mid, hi

    for a in range(3):
        for p in range(PIECES):
            by_y = [
                sides(*[load(9 * a + 3 * b + c, p) for c in range(3)], z0, z7, 1) for b in range(3)
            ]
            for oz in range(3):
                folded = sides(by_y[0][oz], by_y[1][oz], by_y[2][oz], y0, y7, 8)
                for oy in range(3):
                    value = folded[oy]
                    if a != 1:
                        value = rolled(value, 64)
                    parts[a, 3 * oy + oz, :, p * LANES : (p + 1) * LANES] = value

    def part(a, j, p):
        return parts[a, j, :, p * LANES : (p + 1) * LANES]

    def add(slot, p, value):
        at = (slot, rows, slice(p * LANES, (p + 1) * LANES))
        table_grad[at] = table_grad[at] + value

    for j in range(9):
        zero = jnp.zeros((CH, LANES), F32)
        slot = nb_ref[block, 9 + j]
        pieces = []
        for p in range(PIECES):
            low = part(0, j, p)
            if p > 0:
                low = low + part(2, j, p - 1)
            high = part(2, j, p)
            if p < PIECES - 1:
                high = high + part(0, j, p + 1)
            pieces.append(part(1, j, p) + jnp.where(half, low, high))
        whole = (slot, rows, slice(None))
        table_grad[whole] = table_grad[whole] + jnp.concatenate(pieces, axis=1)
        add(nb_ref[block, j], PIECES - 1, jnp.where(half, zero, part(0, j, 0)))
        add(nb_ref[block, 18 + j], 0, jnp.where(half, part(2, j, PIECES - 1), zero))


def level_kernel(
    scale,
    nb_ref,
    live_ref,
    table_hbm,
    cot_ref,
    w_ref,
    wt_ref,
    lift_ref,
    liftt_ref,
    drop_ref,
    dropt_ref,
    out_ref,
    tg_ref,
    wg_ref,
    table,
    cols_hi,
    cols_lo,
    dcols,
    parts,
    wsplit,
    wtsplit,
    acc,
    grad3,
    sem,
):
    slots = table_hbm.shape[0]
    count, chans = cot_ref.shape[:2]
    fetch = pltpu.make_async_copy(table_hbm, table.at[pl.ds(0, slots)], sem)
    fetch.start()
    table[slots] = jnp.zeros((chans, VOX), F32)
    tg_ref[...] = jnp.zeros_like(tg_ref)
    acc[...] = jnp.zeros_like(acc)
    w_hi, w_lo = split(w_ref[...])
    wsplit[:chans] = w_hi
    wsplit[chans:] = w_lo
    wt_hi, wt_lo = split(wt_ref[...])
    wtsplit[...] = jnp.concatenate(
        [wt_hi.astype(F32), wt_lo.astype(F32), wt_hi.astype(F32)], axis=1
    ).astype(BF16)

    lane = lax.broadcasted_iota(jnp.int32, (CH, LANES), 1)
    y, z = (lane // 8) % 8, lane % 8
    masks = (lane < 64, y == 0, y == 7, z == 0, z == 7)

    def spot(v):
        return (v // 128) * 16 + ((v // 16) % 4) * 4 + (v % 8) // 2

    pool = (
        spot(lax.broadcasted_iota(jnp.int32, (VOX, 64), 0))
        == lax.broadcasted_iota(jnp.int32, (VOX, 64), 1)
    ).astype(F32).astype(BF16)
    spread = (
        lax.broadcasted_iota(jnp.int32, (64, VOX), 0)
        == spot(lax.broadcasted_iota(jnp.int32, (64, VOX), 1))
    ).astype(F32).astype(BF16)

    def times(x, m):
        hi, lo = split(x)
        return dot(hi, m) + dot(lo, m)

    def exact(a, b):
        return jnp.dot(a, b, preferred_element_type=F32, precision=HIGH)

    fetch.wait()

    def one_block(b, _):
        def build(c, _):
            rows = pl.ds(pl.multiple_of(c * CH, CH), CH)

            def store(k, p, value):
                hi, lo = split(value)
                at = (pl.ds(pl.multiple_of(k * chans + c * CH, CH), CH), slice(p * LANES, (p + 1) * LANES))
                cols_hi[at] = hi
                cols_lo[at] = lo

            gather_patch(nb_ref, b, table, rows, masks, store)
            return 0

        lax.fori_loop(0, chans // CH, build, 0)
        both = dot(wsplit[...], cols_hi[...])
        pre = both[:chans] + both[chans:] + dot(wsplit[:chans], cols_lo[...])
        live = live_ref[b]
        sig = 1.0 / (1.0 + jnp.exp(-pre))
        hidden = pre * sig
        pooled = times(hidden * live, pool) * 0.125
        lifted_pre = exact(lift_ref[...], pooled)
        lift_sig = 1.0 / (1.0 + jnp.exp(-lifted_pre))
        coarse = exact(drop_ref[...], lifted_pre * lift_sig)
        out_ref[b] = live * (hidden + times(coarse, spread))
        out_grad = live * cot_ref[b]
        coarse_grad = times(out_grad, pool)
        lifted_grad = exact(dropt_ref[...], coarse_grad)
        lifted_pre_grad = lifted_grad * lift_sig * (1.0 + lifted_pre * (1.0 - lift_sig))
        pooled_grad = exact(liftt_ref[...], lifted_pre_grad)
        hidden_grad = out_grad + live * times(pooled_grad, spread) * 0.125
        pre_grad = hidden_grad * sig * (1.0 + pre * (1.0 - sig))
        g_hi, g_lo = split(pre_grad)
        grad3[:chans] = g_hi
        grad3[chans : 2 * chans] = g_hi
        grad3[2 * chans :] = g_lo
        both = dot_nt(grad3[chans:], cols_hi[...])
        acc[...] += both[:chans] + both[chans:] + dot_nt(grad3[:chans], cols_lo[...])

        def fold(c, _):
            rows = pl.ds(pl.multiple_of(c * CH, CH), CH)
            own = pl.ds(pl.multiple_of(c * (K * CH), CH), K * CH)
            dcols[...] = dot(wtsplit[own], grad3[...])

            def load(k, p):
                return dcols[k * CH : (k + 1) * CH, p * LANES : (p + 1) * LANES]

            scatter_patch(nb_ref, b, dcols, parts, tg_ref, rows, masks, load)
            return 0

        lax.fori_loop(0, chans // CH, fold, 0)
        return 0

    lax.fori_loop(0, count, one_block, 0)
    for k in range(K):
        wg_ref[k] = acc[:, k * chans : (k + 1) * chans] * scale


def level(nb, live, table, cot, weight, lift, drop, scale):
    count, chans = cot.shape[:2]
    slots = table.shape[0]
    w = weight.transpose(1, 0, 2).reshape(chans, K * chans)
    wt = weight.reshape(K, chans, chans // CH, CH).transpose(2, 0, 3, 1).reshape(K * chans, chans)
    smem = pl.BlockSpec(memory_space=pltpu.SMEM)
    vmem = pl.BlockSpec(memory_space=pltpu.VMEM)
    return pl.pallas_call(
        functools.partial(level_kernel, scale),
        out_shape=(
            jax.ShapeDtypeStruct((count, chans, VOX), F32),
            jax.ShapeDtypeStruct((slots + 1, chans, VOX), F32),
            jax.ShapeDtypeStruct((K, chans, chans), F32),
        ),
        in_specs=[smem, smem, pl.BlockSpec(memory_space=pl.ANY)] + [vmem] * 7,
        out_specs=(vmem, vmem, vmem),
        scratch_shapes=[
            pltpu.VMEM((slots + 1, chans, VOX), F32),
            pltpu.VMEM((K * chans, VOX), BF16),
            pltpu.VMEM((K * chans, VOX), BF16),
            pltpu.VMEM((K * CH, VOX), F32),
            pltpu.VMEM((3, 9, CH, VOX), F32),
            pltpu.VMEM((2 * chans, K * chans), BF16),
            pltpu.VMEM((K * chans, 3 * chans), BF16),
            pltpu.VMEM((chans, K * chans), F32),
            pltpu.VMEM((3 * chans, VOX), BF16),
            pltpu.SemaphoreType.DMA,
        ],
        compiler_params=pltpu.CompilerParams(vmem_limit_bytes=48 * 1024 * 1024),
        name="level",
    )(nb, live, table, cot, w, wt, lift, lift.T, drop, drop.T)


def shifted(array, by):
    length = lax.axis_size("slab")
    pairs = [(i, i + by) for i in range(length) if 0 <= i + by < length]
    return lax.ppermute(array, "slab", pairs)


def shards(features, block_count, neighbours, conv_weight, lift_weight, drop_weight, cotangent):
    blocks = features.shape[0]
    subs = lax.axis_size("sub")
    count = blocks // subs
    first = lax.axis_index("sub") * count
    narrow = jnp.concatenate([shifted(features, 1), features, shifted(features, -1)], axis=0)
    table = lax.all_gather(narrow, "sub", axis=1, tiled=True)
    cot = lax.all_to_all(cotangent, "sub", 0, 1, tiled=True)
    weight = lax.all_gather(conv_weight, "sub", axis=1, tiled=True)
    drop = lax.all_gather(drop_weight, "sub", axis=0, tiled=True)
    nb = lax.dynamic_slice_in_dim(neighbours, first, count, 0)
    live = (first + lax.iota(jnp.int32, count) < block_count[0]).astype(F32)
    scale = float((VOX * blocks * lax.axis_size("slab")) ** -0.5)
    out, table_grad, weight_part = level(nb, live, table, cot, weight, lift_weight, drop, scale)
    output = lax.all_to_all(out, "sub", 1, 0, tiled=True)
    mine = lax.psum_scatter(table_grad[: 3 * blocks], "sub", scatter_dimension=1, tiled=True)
    feature_grad = (
        mine[blocks : 2 * blocks]
        + shifted(mine[:blocks], -1)
        + shifted(mine[2 * blocks :], 1)
    )
    own = lax.psum_scatter(weight_part, "sub", scatter_dimension=1, tiled=True)
    weight_grad = lax.psum(own, "slab")
    return (output, feature_grad, weight_grad)


def solution(mesh):
    return jax.shard_map(
        shards,
        mesh=mesh,
        in_specs=(
            P(("groups", "slab"), "sub", None),
            P(("groups", "slab")),
            P(("groups", "slab"), None),
            P(None, "sub", None),
            P(),
            P("sub", None),
            P(("groups", "slab"), "sub", None),
        ),
        out_specs=(
            P(("groups", "slab"), "sub", None),
            P(("groups", "slab"), "sub", None),
            P(None, ("groups", "sub"), None),
        ),
        check_vma=False,
    )
```

time: 1890 us -> 236 us (0.12)
  local copies, waits for them, and re-layouts: 1300 us -> 14.3 us
  other arithmetic: 247 us -> 4.4 us
  matrix products: 135 us -> 0 us
  Pallas kernels: 0 us -> 67.5 us
  waiting for transfers between devices: 141 us -> 111 us
  loops' own time: 20 us -> 0 us
    another operation x249 -> x0, local copies, waits for them, and re-layouts: 413 us -> none  [the longest x248 410 us: single(): jnp.stack([patch[:, a:a + 8, b:b + 8, c:c + 8].reshape(chans, 512) for a...]
    while x625 -> x0, local copies, waits for them, and re-layouts: 291 us -> none
    reshape x441 -> x1, local copies, waits for them, and re-layouts: 279 us -> 1.55 us  [level(): w = weight.transpose(1, 0, 2).reshape(chans, K * chans)]
    slice x177 -> x2, local copies, waits for them, and re-layouts: 222 us -> 5.32 us  [the longest x1 4.03 us: shards(): table_grad[:3 * blocks]]
    dot_general x28 -> x0, matrix products: 135 us -> none  [the longest x24 131 us: single(): return jnp.einsum('koi,kiv->ov', weight, cols, precision=HIGH)]
    concatenate x65 -> x1, other arithmetic: 83.8 us -> 2.39 us  [shards(): jnp.concatenate([shifted(features, 1), features, shifted(features, -1)],...]
    scatter-add x8 -> x0, other arithmetic: 74.5 us -> none  [single(): near = table[row].reshape(3, 3, 3, chans, 8, 8, 8)]
    add_any x32 -> x0, other arithmetic: 67.7 us -> none  [the longest x8 33.7 us: single(): patch[:, a:a + 8, b:b + 8, c:c + 8].reshape(chans, 512)]
  transfers between devices with their start and end apart: 8 -> 9, of which waited for: 6 -> 6; matrix products, arithmetic and copies ran while one was open for 0% -> 4% of each run, Pallas kernels for 0% -> 0%
where the time goes in v1:
time: 236 us
  waiting for transfers between devices  111 us (47%)
  Pallas kernels  67.5 us (29%)
  starting transfers between devices  15.9 us (7%)
  between operations  14.6 us (6%)
  local copies, waits for them, and re-layouts  14.3 us (6%)
  blocking collectives  8.42 us (4%)
  other arithmetic  4.4 us (2%)
    pallas_call x1, Pallas kernels, level(): pl.pallas_call(functools.partial(level_kernel, scale), out_shape=(jax.Sha...  67.5 us
    psum x1, waiting for transfers between devices, shards(): weight_grad = lax.psum(own, 'slab')  57.5 us
    ppermute x4, waiting for transfers between devices, shifted(): return lax.ppermute(array, 'slab', pairs)  39 us
    reduce_scatter x1, waiting for transfers between devices, shards(): lax.psum_scatter(table_grad[:3 * blocks], 'sub', scatter_dimension=1, til...  12.3 us
    ppermute x4, starting transfers between devices, shifted(): return lax.ppermute(array, 'slab', pairs)  12.1 us
  transfers between devices with their start and end apart: 9, of which 6 were waited for; matrix products, arithmetic and copies ran while one was open for 4% of the time, Pallas kernels for 0%

profile of v1, /device:TPU:0, one launch (start us, length us, event | category | flops | bytes accessed | tf_op | source)
XLA Modules:
  0.0 235.7 jit_solution(12370171173560943291)
XLA Ops:
  7.2 4.9 %collective-permute-start = (f32[8,32,512]{2,1,0:T(8,128)}, f32[8,32,512]{2,1,0:T(8,128)S(1)}, u32[]{:S(2)}, u32[]{:S(2)}) collective-permute-start(f32[8,32,512]{2,1,0:T(8,128)} %param.7), channel_id=1, source_target_pairs={{0,2},{2,4},{4,6},{6,8},{8,10},{10,12},{12,14},{1,3},{3,5},{5,7},{... | collective-permute-start | bytes 1572872 | tf_op jit(solution)/shard_map/ppermute | solution.py:280
  12.1 1.3 collective-permute-start.1
  13.4 21.4 %collective-permute-done = f32[8,32,512]{2,1,0:T(8,128)S(1)} collective-permute-done((f32[8,32,512]{2,1,0:T(8,128)}, f32[8,32,512]{2,1,0:T(8,128)S(1)}, u32[]{:S(2)}, u32[]{:S(2)}) %collective-permute-start) | collective-permute-done | bytes 524320 | tf_op jit(solution)/shard_map/ppermute | solution.py:280
  34.8 2.4 %pad_maximum_fusion = f32[24,32,512]{2,1,0:T(8,128)} fusion(f32[8,32,512]{2,1,0:T(8,128)S(1)} %collective-permute-done.1, f32[8,32,512]{2,1,0:T(8,128)} %param.7, f32[8,32,512]{2,1,0:T(8,128)S(1)} %collective-permute-done), kind=kLoop, calls=%fused_computation | loop fusion | flops 786432 | bytes 3145728 | tf_op jit(solution)/shard_map/concatenate | solution.py:288
  37.2 3.6 %all-to-all-start = ((f32[8,32,512]{2,1,0:T(8,128)}), f32[8,32,512]{2,1,0:T(8,128)S(1)}, u32[]{:S(2)}, u32[]{:S(2)}) async-start(f32[8,32,512]{2,1,0:T(8,128)} %param.13), calls=%async_computation | async-start | bytes 1048576 | tf_op jit(solution)/shard_map/all_to_all | solution.py:290
  40.9 0.0 reduce-scatter.3.cloned.1.call-start
  41.6 1.0 all-to-all-done
  42.7 1.8 all_gather.11.drop_ref
  44.5 0.1 copy.29
  44.6 0.1 copy.30.lift_ref
  44.7 2.4 %all_gather.10 = f32[27,64,64]{2,1,0:T(8,128)S(1)} all-gather(f32[27,32,64]{2,1,0:T(8,128)S(1)} %copy-done.2), channel_id=1, replica_groups=mesh['groups'=2,'slab'=8,'sub'=2] {'sub'}, dimensions={1}, use_global_device_ids=true | all-gather | bytes 663552 | tf_op jit(solution)/shard_map/all_gather | solution.py:291
  47.1 1.2 copy.27
  48.4 1.4 copy.28
  49.7 1.5 copy.26
  51.3 1.5 reshape.15.w_ref
  52.9 67.5 %level.1 = (f32[4,64,512]{2,1,0:T(8,128)S(1)}, f32[25,64,512]{2,1,0:T(8,128)}, f32[27,64,64]{2,1,0:T(8,128)}) custom-call(s32[4,27]{1,0:T(4,128)S(1)} %constant_dynamic-slice_fusion.nb_ref, f32[4]{0:T(128)S(1)} %compare_convert_fusion.live_ref, f32[24,64,512]{2,1,0:T(8,128)} %all-gather.2.cloned.1.call-done.table_hbm, f32[4,64,512]{2,1,0:T(8,128)S(1)} %bitcast.18, ...), custom_call_target="tpu_custom_call" | custom-call | tf_op jit(solution)/shard_map/level/pallas_call | solution.py:251
  120.4 4.0 %slice.12 = f32[24,64,512]{2,1,0:T(8,128)} slice(f32[25,64,512]{2,1,0:T(8,128)} %get-tuple-element.7), slice={[0:24], [0:64], [0:512]} | slice | bytes 6291456 | tf_op jit(solution)/shard_map/slice | solution.py:298
  124.4 0.0 reduce-scatter.5.cloned.1.call-start
  124.5 0.7 reduce-scatter.5.cloned.1.call-update
  125.2 0.0 all-reduce.2.cloned.1.call-start
  125.2 12.3 %reduce-scatter.3.cloned.1.call-done = f32[24,32,512]{2,1,0:T(8,128)} async-done(((f32[24,64,512]{2,1,0:T(8,128)}), f32[24,32,512]{2,1,0:T(8,128)}) %reduce-scatter.3.cloned.1.call-update) | async-done | bytes 1572880 | tf_op jit(solution)/shard_map/reduce_scatter | solution.py:298
  137.5 1.3 fusion.1
  138.8 1.3 collective-permute-start.2
  140.1 4.6 %collective-permute-start.3 = (f32[8,32,512]{2,1,0:T(8,128)S(1)}, f32[8,32,512]{2,1,0:T(8,128)S(1)}, u32[]{:S(2)}, u32[]{:S(2)}) collective-permute-start(f32[8,32,512]{2,1,0:T(8,128)S(1)} %get-tuple-element.10), channel_id=1, source_target_pairs={{0,2},{2,4},{4,6},{6,8},{8,10},{10,12},{12,14},{1,3},{3,5},{5,7},{... | collective-permute-start | bytes 1572872 | tf_op jit(solution)/shard_map/ppermute | solution.py:280
  144.7 0.3 copy.31
  145.1 4.2 %all_to_all.36 = f32[4,64,512]{2,0,1:T(4,128)S(1)} all-to-all(f32[4,64,512]{2,0,1:T(4,128)S(1)} %copy.31), channel_id=1, replica_groups=mesh['groups'=2,'slab'=8,'sub'=2] {'sub'}, dimensions={1} | all-to-all | bytes 1048576 | tf_op jit(solution)/shard_map/all_to_all | solution.py:297
  149.2 1.0 copy.32
  150.2 4.7 %collective-permute-done.2 = f32[8,32,512]{2,1,0:T(8,128)S(1)} collective-permute-done((f32[8,32,512]{2,1,0:T(8,128)S(1)}, f32[8,32,512]{2,1,0:T(8,128)S(1)}, u32[]{:S(2)}, u32[]{:S(2)}) %collective-permute-start.2) | collective-permute-done | bytes 524320 | tf_op jit(solution)/shard_map/ppermute | solution.py:280
  154.9 13.0 %collective-permute-done.3 = f32[8,32,512]{2,1,0:T(8,128)S(1)} collective-permute-done((f32[8,32,512]{2,1,0:T(8,128)S(1)}, f32[8,32,512]{2,1,0:T(8,128)S(1)}, u32[]{:S(2)}, u32[]{:S(2)}) %collective-permute-start.3) | collective-permute-done | bytes 524320 | tf_op jit(solution)/shard_map/ppermute | solution.py:280
  167.8 2.0 fusion
  169.8 57.5 %all-reduce.2.cloned.1.call-done = f32[27,32,64]{2,1,0:T(8,128)} async-done(((f32[27,32,64]{2,1,0:T(8,128)}), f32[27,32,64]{2,1,0:T(8,128)}) %all-reduce.2.cloned.1.call-update) | async-done | bytes 221200 | tf_op jit(solution)/shard_map/psum | solution.py:305
  227.4 1.8 copy.35
  (18 shorter events, 0.2 us)
Async XLA Ops:
  7.2 45.7 %copy-start = (s32[8,27]{1,0:T(8,128)S(1)}, s32[8,27]{1,0:T(8,128)}, u32[]{:S(2)}) copy-start(s32[8,27]{1,0:T(8,128)} %param.9) | copy-start | bytes 2596
  7.2 45.7 %all-gather.2.cloned.1.call-start = ((), (), s32[]{:S(2)}) async-start(), calls=%async_computation.4 | async-start | bytes 4718592 | tf_op jit(solution)/shard_map/all_gather | solution.py:289
  7.2 27.6 %collective-permute-start = (f32[8,32,512]{2,1,0:T(8,128)}, f32[8,32,512]{2,1,0:T(8,128)S(1)}, u32[]{:S(2)}, u32[]{:S(2)}) collective-permute-start(f32[8,32,512]{2,1,0:T(8,128)} %param.7), channel_id=1, source_target_pairs={{0,2},{2,4},{4,6},{6,8},{8,10},{10,12},{12,14},{1,3},{3,5},{5,7},{... | collective-permute-start | bytes 1572872 | tf_op jit(solution)/shard_map/ppermute | solution.py:280
  12.1 22.7 %collective-permute-start.1 = (f32[8,32,512]{2,1,0:T(8,128)}, f32[8,32,512]{2,1,0:T(8,128)S(1)}, u32[]{:S(2)}, u32[]{:S(2)}) collective-permute-start(f32[8,32,512]{2,1,0:T(8,128)} %param.7), channel_id=1, source_target_pairs={{2,0},{4,2},{6,4},{8,6},{10,8},{12,10},{14,12},{3,1},{5,3},{7,5},{... | collective-permute-start | bytes 1572872 | tf_op jit(solution)/shard_map/ppermute | solution.py:280
  37.2 5.4 %copy-start.3 = (f32[32,128]{1,0:T(8,128)S(1)}, f32[32,128]{1,0:T(8,128)}, u32[]{:S(2)}) copy-start(f32[32,128]{1,0:T(8,128)} %param.12) | copy-start | bytes 49156
  37.2 7.4 %copy-start.1 = (f32[128,64]{0,1:T(8,128)S(1)}, f32[128,64]{0,1:T(8,128)}, u32[]{:S(2)}) copy-start(f32[128,64]{0,1:T(8,128)} %param.11) | copy-start | bytes 98308
  37.2 7.5 %copy-start.2 = (f32[27,32,64]{2,1,0:T(8,128)S(1)}, f32[27,32,64]{2,1,0:T(8,128)}, u32[]{:S(2)}) copy-start(f32[27,32,64]{2,1,0:T(8,128)} %param.10) | copy-start | bytes 663556
  37.2 5.4 %all-to-all-start = ((f32[8,32,512]{2,1,0:T(8,128)}), f32[8,32,512]{2,1,0:T(8,128)S(1)}, u32[]{:S(2)}, u32[]{:S(2)}) async-start(f32[8,32,512]{2,1,0:T(8,128)} %param.13), calls=%async_computation | async-start | bytes 1048576 | tf_op jit(solution)/shard_map/all_to_all | solution.py:290
  40.9 96.7 %reduce-scatter.3.cloned.1.call-start = ((), (), s32[]{:S(2)}) async-start(), calls=%async_computation.5 | async-start | bytes 4718592 | tf_op jit(solution)/shard_map/reduce_scatter | solution.py:298
  124.4 25.8 %reduce-scatter.5.cloned.1.call-start = ((), (), s32[]{:S(2)}) async-start(), calls=%async_computation.6 | async-start | bytes 1327104 | tf_op jit(solution)/shard_map/reduce_scatter | solution.py:304
  125.2 102.2 %all-reduce.2.cloned.1.call-start = ((), (), s32[]{:S(2)}) async-start(), calls=%async_computation.7 | async-start | bytes 884736 | tf_op jit(solution)/shard_map/psum | solution.py:305
  138.8 16.0 %collective-permute-start.2 = (f32[8,32,512]{2,1,0:T(8,128)S(1)}, f32[8,32,512]{2,1,0:T(8,128)S(1)}, u32[]{:S(2)}, u32[]{:S(2)}) collective-permute-start(f32[8,32,512]{2,1,0:T(8,128)S(1)} %get-tuple-element.9), channel_id=1, source_target_pairs={{2,0},{4,2},{6,4},{8,6},{10,8},{12,10},{14,12},{3,1},{5,3},{7,5},{... | collective-permute-start | bytes 1572872 | tf_op jit(solution)/shard_map/ppermute | solution.py:280
  140.1 27.7 %collective-permute-start.3 = (f32[8,32,512]{2,1,0:T(8,128)S(1)}, f32[8,32,512]{2,1,0:T(8,128)S(1)}, u32[]{:S(2)}, u32[]{:S(2)}) collective-permute-start(f32[8,32,512]{2,1,0:T(8,128)S(1)} %get-tuple-element.10), channel_id=1, source_target_pairs={{0,2},{2,4},{4,6},{6,8},{8,10},{10,12},{12,14},{1,3},{3,5},{5,7},{... | collective-permute-start | bytes 1572872 | tf_op jit(solution)/shard_map/ppermute | solution.py:280
Sparse Core Ops, SparseCore 0:
  37.4 14.1 all-gather.1
  124.5 12.9 reduce-scatter.2
  139.9 9.4 reduce-scatter.4
  153.1 74.2 all-reduce.1

commit v2 on v1

--- a/solution.py
+++ b/solution.py
@@ -118,50 +118,53 @@
         add(nb_ref[block, 18 + j], 0, jnp.where(half, part(2, j, PIECES - 1), zero))
 
 
-def level_kernel(
+def lane_masks():
+    lane = lax.broadcasted_iota(jnp.int32, (CH, LANES), 1)
+    y, z = (lane // 8) % 8, lane % 8
+    return lane < 64, y == 0, y == 7, z == 0, z == 7
+
+
+def forward_kernel(
     scale,
     nb_ref,
     live_ref,
-    table_hbm,
+    below_ref,
+    below_x_ref,
+    own_ref,
+    own_x_ref,
+    above_ref,
+    above_x_ref,
     cot_ref,
+    cot_x_ref,
     w_ref,
-    wt_ref,
     lift_ref,
     liftt_ref,
     drop_ref,
     dropt_ref,
     out_ref,
-    tg_ref,
+    out_x_ref,
+    grad_ref,
     wg_ref,
+    wg_x_ref,
     table,
     cols_hi,
     cols_lo,
-    dcols,
-    parts,
     wsplit,
-    wtsplit,
     acc,
-    grad3,
-    sem,
 ):
-    slots = table_hbm.shape[0]
-    count, chans = cot_ref.shape[:2]
-    fetch = pltpu.make_async_copy(table_hbm, table.at[pl.ds(0, slots)], sem)
-    fetch.start()
-    table[slots] = jnp.zeros((chans, VOX), F32)
-    tg_ref[...] = jnp.zeros_like(tg_ref)
+    count, half = cot_ref.shape[:2]
+    chans = 2 * half
+    blocks = own_ref.shape[0]
+    sources = ((below_ref, below_x_ref), (own_ref, own_x_ref), (above_ref, above_x_ref))
+    for i, (first, second) in enumerate(sources):
+        table[i * blocks : (i + 1) * blocks, :half] = first[...]
+        table[i * blocks : (i + 1) * blocks, half:] = second[...]
+    table[3 * blocks] = jnp.zeros((chans, VOX), F32)
     acc[...] = jnp.zeros_like(acc)
     w_hi, w_lo = split(w_ref[...])
     wsplit[:chans] = w_hi
     wsplit[chans:] = w_lo
-    wt_hi, wt_lo = split(wt_ref[...])
-    wtsplit[...] = jnp.concatenate(
-        [wt_hi.astype(F32), wt_lo.astype(F32), wt_hi.astype(F32)], axis=1
-    ).astype(BF16)
-
-    lane = lax.broadcasted_iota(jnp.int32, (CH, LANES), 1)
-    y, z = (lane // 8) % 8, lane % 8
-    masks = (lane < 64, y == 0, y == 7, z == 0, z == 7)
+    masks = lane_masks()
 
     def spot(v):
         return (v // 128) * 16 + ((v // 16) % 4) * 4 + (v % 8) // 2
@@ -182,15 +185,16 @@
     def exact(a, b):
         return jnp.dot(a, b, preferred_element_type=F32, precision=HIGH)
 
-    fetch.wait()
-
     def one_block(b, _):
         def build(c, _):
             rows = pl.ds(pl.multiple_of(c * CH, CH), CH)
 
             def store(k, p, value):
                 hi, lo = split(value)
-                at = (pl.ds(pl.multiple_of(k * chans + c * CH, CH), CH), slice(p * LANES, (p + 1) * LANES))
+                at = (
+                    pl.ds(pl.multiple_of(k * chans + c * CH, CH), CH),
+                    slice(p * LANES, (p + 1) * LANES),
+                )
                 cols_hi[at] = hi
                 cols_lo[at] = lo
 
@@ -207,8 +211,10 @@
         lifted_pre = exact(lift_ref[...], pooled)
         lift_sig = 1.0 / (1.0 + jnp.exp(-lifted_pre))
         coarse = exact(drop_ref[...], lifted_pre * lift_sig)
-        out_ref[b] = live * (hidden + times(coarse, spread))
-        out_grad = live * cot_ref[b]
+        out = live * (hidden + times(coarse, spread))
+        out_ref[b] = out[:half]
+        out_x_ref[b] = out[half:]
+        out_grad = live * jnp.concatenate([cot_ref[b], cot_x_ref[b]], axis=0)
         coarse_grad = times(out_grad, pool)
         lifted_grad = exact(dropt_ref[...], coarse_grad)
         lifted_pre_grad = lifted_grad * lift_sig * (1.0 + lifted_pre * (1.0 - lift_sig))
@@ -216,62 +222,112 @@
         hidden_grad = out_grad + live * times(pooled_grad, spread) * 0.125
         pre_grad = hidden_grad * sig * (1.0 + pre * (1.0 - sig))
         g_hi, g_lo = split(pre_grad)
-        grad3[:chans] = g_hi
-        grad3[chans : 2 * chans] = g_hi
-        grad3[2 * chans :] = g_lo
-        both = dot_nt(grad3[chans:], cols_hi[...])
-        acc[...] += both[:chans] + both[chans:] + dot_nt(grad3[:chans], cols_lo[...])
-
+        g_both = jnp.concatenate([g_hi, g_lo], axis=0)
+        grad_ref[b] = jnp.concatenate([g_hi, g_both], axis=0)
+        both = dot_nt(g_both, cols_hi[...])
+        acc[...] += both[:chans] + both[chans:] + dot_nt(g_hi, cols_lo[...])
+        return 0
+
+    lax.fori_loop(0, count, one_block, 0)
+    for k in range(K):
+        wg_ref[k] = acc[:half, k * chans : (k + 1) * chans] * scale
+        wg_x_ref[k] = acc[half:, k * chans : (k + 1) * chans] * scale
+
+
+def backward_kernel(nb_ref, grad_ref, wt_ref, tg_ref, tg_x_ref, total, dcols, parts, wtsplit):
+    count = grad_ref.shape[0]
+    slots, half = tg_ref.shape[:2]
+    chans = 2 * half
+    total[...] = jnp.zeros_like(total)
+    wt_hi, wt_lo = split(wt_ref[...])
+    wtsplit[...] = jnp.concatenate(
+        [wt_hi.astype(F32), wt_lo.astype(F32), wt_hi.astype(F32)], axis=1
+    ).astype(BF16)
+    masks = lane_masks()
+
+    def one_block(b, _):
         def fold(c, _):
             rows = pl.ds(pl.multiple_of(c * CH, CH), CH)
             own = pl.ds(pl.multiple_of(c * (K * CH), CH), K * CH)
-            dcols[...] = dot(wtsplit[own], grad3[...])
+            dcols[...] = dot(wtsplit[own], grad_ref[b])
 
             def load(k, p):
                 return dcols[k * CH : (k + 1) * CH, p * LANES : (p + 1) * LANES]
 
-            scatter_patch(nb_ref, b, dcols, parts, tg_ref, rows, masks, load)
+            scatter_patch(nb_ref, b, dcols, parts, total, rows, masks, load)
             return 0
 
         lax.fori_loop(0, chans // CH, fold, 0)
         return 0
 
     lax.fori_loop(0, count, one_block, 0)
-    for k in range(K):
-        wg_ref[k] = acc[:, k * chans : (k + 1) * chans] * scale
-
-
-def level(nb, live, table, cot, weight, lift, drop, scale):
-    count, chans = cot.shape[:2]
-    slots = table.shape[0]
+    tg_ref[...] = total[:slots, :half]
+    tg_x_ref[...] = total[:slots, half:]
+
+
+SMEM = pl.BlockSpec(memory_space=pltpu.SMEM)
+VMEM = pl.BlockSpec(memory_space=pltpu.VMEM)
+
+
+def params(mib):
+    return pltpu.CompilerParams(vmem_limit_bytes=mib * 1024 * 1024)
+
+
+def cost(us):
+    return pl.CostEstimate(flops=us * 10**9, bytes_accessed=us * 3 * 10**6, transcendentals=0)
+
+
+def level_forward(nb, live, table, cot, weight, lift, drop, scale):
+    count, half = cot[0].shape[:2]
+    chans = 2 * half
+    slots = 3 * table[0].shape[0]
     w = weight.transpose(1, 0, 2).reshape(chans, K * chans)
-    wt = weight.reshape(K, chans, chans // CH, CH).transpose(2, 0, 3, 1).reshape(K * chans, chans)
-    smem = pl.BlockSpec(memory_space=pltpu.SMEM)
-    vmem = pl.BlockSpec(memory_space=pltpu.VMEM)
+    part = jax.ShapeDtypeStruct((count, half, VOX), F32)
+    weight_part = jax.ShapeDtypeStruct((K, half, chans), F32)
     return pl.pallas_call(
-        functools.partial(level_kernel, scale),
+        functools.partial(forward_kernel, scale),
         out_shape=(
-            jax.ShapeDtypeStruct((count, chans, VOX), F32),
-            jax.ShapeDtypeStruct((slots + 1, chans, VOX), F32),
-            jax.ShapeDtypeStruct((K, chans, chans), F32),
+            part,
+            part,
+            jax.ShapeDtypeStruct((count, 3 * chans, VOX), BF16),
+            weight_part,
+            weight_part,
         ),
-        in_specs=[smem, smem, pl.BlockSpec(memory_space=pl.ANY)] + [vmem] * 7,
-        out_specs=(vmem, vmem, vmem),
+        in_specs=[SMEM, SMEM] + [VMEM] * 13,
+        out_specs=(VMEM,) * 5,
         scratch_shapes=[
             pltpu.VMEM((slots + 1, chans, VOX), F32),
             pltpu.VMEM((K * chans, VOX), BF16),
             pltpu.VMEM((K * chans, VOX), BF16),
+            pltpu.VMEM((2 * chans, K * chans), BF16),
+            pltpu.VMEM((chans, K * chans), F32),
+        ],
+        compiler_params=params(40),
+        cost_estimate=cost(35),
+        name="level_forward",
+    )(nb, live, *table, *cot, w, lift, lift.T, drop, drop.T)
+
+
+def level_backward(nb, grad, weight, slots):
+    chans = weight.shape[1]
+    half = chans // 2
+    wt = weight.reshape(K, chans, chans // CH, CH).transpose(2, 0, 3, 1).reshape(K * chans, chans)
+    part = jax.ShapeDtypeStruct((slots, half, VOX), F32)
+    return pl.pallas_call(
+        backward_kernel,
+        out_shape=(part, part),
+        in_specs=[SMEM, VMEM, VMEM],
+        out_specs=(VMEM, VMEM),
+        scratch_shapes=[
+            pltpu.VMEM((slots + 1, chans, VOX), F32),
             pltpu.VMEM((K * CH, VOX), F32),
             pltpu.VMEM((3, 9, CH, VOX), F32),
-            pltpu.VMEM((2 * chans, K * chans), BF16),
             pltpu.VMEM((K * chans, 3 * chans), BF16),
-            pltpu.VMEM((chans, K * chans), F32),
-            pltpu.VMEM((3 * chans, VOX), BF16),
-            pltpu.SemaphoreType.DMA,
         ],
-        compiler_params=pltpu.CompilerParams(vmem_limit_bytes=48 * 1024 * 1024),
-        name="level",
-    )(nb, live, table, cot, w, wt, lift, lift.T, drop, drop.T)
+        compiler_params=params(40),
+        cost_estimate=cost(30),
+        name="level_backward",
+    )(nb, grad, wt)
 
 
 def shifted(array, by):
@@ -280,29 +336,57 @@
     return lax.ppermute(array, "slab", pairs)
 
 
+def swap(array):
+    return lax.ppermute(array, "sub", [(0, 1), (1, 0)])
+
+
+def slab_sum(array):
+    length = lax.axis_size("slab")
+    if length & (length - 1):
+        return lax.psum(array, "slab")
+    step = 1
+    while step < length:
+        array = array + lax.ppermute(array, "slab", [(i, i ^ step) for i in range(length)])
+        step *= 2
+    return array
+
+
 def shards(features, block_count, neighbours, conv_weight, lift_weight, drop_weight, cotangent):
-    blocks = features.shape[0]
-    subs = lax.axis_size("sub")
-    count = blocks // subs
-    first = lax.axis_index("sub") * count
-    narrow = jnp.concatenate([shifted(features, 1), features, shifted(features, -1)], axis=0)
-    table = lax.all_gather(narrow, "sub", axis=1, tiled=True)
-    cot = lax.all_to_all(cotangent, "sub", 0, 1, tiled=True)
-    weight = lax.all_gather(conv_weight, "sub", axis=1, tiled=True)
-    drop = lax.all_gather(drop_weight, "sub", axis=0, tiled=True)
+    blocks, half = features.shape[:2]
+    sub = lax.axis_index("sub")
+    lead = sub == 0
+    count = blocks // 2
+    first = sub * count
+
+    def own_first(array, axis):
+        return jnp.where(lead, array, jnp.roll(array, half, axis=axis))
+
+    below, above = shifted(features, 1), shifted(features, -1)
+    table = (below, swap(below), features, swap(features), above, swap(above))
+    cot = (
+        lax.dynamic_slice_in_dim(cotangent, first, count, 0),
+        swap(lax.dynamic_slice_in_dim(cotangent, count - first, count, 0)),
+    )
+    weight = own_first(jnp.concatenate([conv_weight, swap(conv_weight)], axis=1), 2)
+    drop = jnp.concatenate([drop_weight, swap(drop_weight)], axis=0)
     nb = lax.dynamic_slice_in_dim(neighbours, first, count, 0)
     live = (first + lax.iota(jnp.int32, count) < block_count[0]).astype(F32)
     scale = float((VOX * blocks * lax.axis_size("slab")) ** -0.5)
-    out, table_grad, weight_part = level(nb, live, table, cot, weight, lift_weight, drop, scale)
-    output = lax.all_to_all(out, "sub", 1, 0, tiled=True)
-    mine = lax.psum_scatter(table_grad[: 3 * blocks], "sub", scatter_dimension=1, tiled=True)
+    out, out_x, grad, part, part_x = level_forward(
+        nb, live, table, cot, weight, own_first(lift_weight, 1), drop, scale
+    )
+    table_grad, table_grad_x = level_backward(nb, grad, weight, 3 * blocks)
+    received = swap(out_x)
+    output = jnp.concatenate(
+        [jnp.where(lead, out, received), jnp.where(lead, received, out)], axis=0
+    )
+    weight_grad = slab_sum(own_first(part, 2) + swap(own_first(part_x, 2)))
+    mine = table_grad + swap(table_grad_x)
     feature_grad = (
         mine[blocks : 2 * blocks]
         + shifted(mine[:blocks], -1)
         + shifted(mine[2 * blocks :], 1)
     )
-    own = lax.psum_scatter(weight_part, "sub", scatter_dimension=1, tiled=True)
-    weight_grad = lax.psum(own, "slab")
     return (output, feature_grad, weight_grad)
 
 

time: 236 us -> 163 us (0.69)
  waiting for transfers between devices: 111 us -> 53.4 us
  between operations: 14.6 us -> 1.57 us
  blocking collectives: 8.42 us -> 0 us
  starting transfers between devices: 15.9 us -> 22.2 us
  other arithmetic: 4.4 us -> 9.55 us
  local copies, waits for them, and re-layouts: 14.3 us -> 10 us
    psum x1 -> x0, waiting for transfers between devices: 57.5 us -> none  [shards(): weight_grad = lax.psum(own, 'slab')]
    ppermute x0 -> x12, waiting for transfers between devices: none -> 38.3 us  [the longest x3 35.4 us: slab_sum(): lax.ppermute(array, 'slab', [(i, i ^ step) for i in range(length)])]
    ppermute x4, waiting for transfers between devices: 39 us -> 15.1 us  [shifted(): return lax.ppermute(array, 'slab', pairs)]
    reduce_scatter x2 -> x0, waiting for transfers between devices: 12.3 us -> none  [the longest x1 12.3 us: shards(): lax.psum_scatter(table_grad[:3 * blocks], 'sub', scatter_dimension=1, til...]
    ppermute x0 -> x12, starting transfers between devices: none -> 10.4 us  [the longest x3 8.12 us: slab_sum(): lax.ppermute(array, 'slab', [(i, i ^ step) for i in range(length)])]
    all_gather x2 -> x0, blocking collectives: 4.27 us -> none  [the longest x1 2.44 us: shards(): weight = lax.all_gather(conv_weight, 'sub', axis=1, tiled=True)]
    all_to_all x1 -> x0, blocking collectives: 4.15 us -> none  [shards(): output = lax.all_to_all(out, 'sub', 1, 0, tiled=True)]
    all_to_all x1 -> x0, starting transfers between devices: 3.63 us -> none  [shards(): cot = lax.all_to_all(cotangent, 'sub', 0, 1, tiled=True)]
  transfers between devices with their start and end apart: 9 -> 16, of which waited for: 6 -> 5; matrix products, arithmetic and copies ran while one was open for 4% -> 11% of each run, Pallas kernels for 0% -> 0%
where the time goes in v2:
time: 163 us
  Pallas kernels  65.8 us (40%)
  waiting for transfers between devices  53.4 us (33%)
  starting transfers between devices  22.2 us (14%)
  local copies, waits for them, and re-layouts  10 us (6%)
  other arithmetic  9.55 us (6%)
    pallas_call x1, Pallas kernels, level_forward(): pl.pallas_call(functools.partial(forward_kernel, scale), out_shape=(part,...  41.9 us
    ppermute x3, waiting for transfers between devices, slab_sum(): lax.ppermute(array, 'slab', [(i, i ^ step) for i in range(length)])  35.4 us
    pallas_call x1, Pallas kernels, level_backward(): pl.pallas_call(backward_kernel, out_shape=(part, part), in_specs=[SMEM, V...  24 us
    ppermute x4, waiting for transfers between devices, shifted(): return lax.ppermute(array, 'slab', pairs)  15.1 us
    ppermute x4, starting transfers between devices, shifted(): return lax.ppermute(array, 'slab', pairs)  11.8 us
    ppermute x3, starting transfers between devices, slab_sum(): lax.ppermute(array, 'slab', [(i, i ^ step) for i in range(length)])  8.12 us
  transfers between devices with their start and end apart: 16, of which 5 were waited for; matrix products, arithmetic and copies ran while one was open for 11% of the time, Pallas kernels for 0%

profile of v2, /device:TPU:0, one launch (start us, length us, event | category | flops | bytes accessed | tf_op | source)
XLA Modules:
  0.0 162.6 jit_solution(15062070175520401457)
XLA Ops:
  0.7 0.5 collective-permute-start.2
  1.2 4.6 %collective-permute-start = (f32[8,32,512]{2,1,0:T(8,128)}, f32[8,32,512]{2,1,0:T(8,128)S(1)}, u32[]{:S(2)}, u32[]{:S(2)}) collective-permute-start(f32[8,32,512]{2,1,0:T(8,128)} %own_ref.1), channel_id=1, source_target_pairs={{0,2},{2,4},{4,6},{6,8},{8,10},{10,12},{12,14},{1,3},{3,5},{5,7},{... | collective-permute-start | bytes 1572872 | tf_op jit(solution)/shard_map/ppermute | solution.py:336
  5.8 1.3 collective-permute-start.3
  7.1 0.8 copy.32
  8.0 0.4 collective-permute-start.6
  9.1 1.8 %constant_dynamic-slice_fusion = (f32[4,32,512]{2,1,0:T(8,128)}, f32[4,32,512]{2,1,0:T(8,128)S(1)}) fusion(f32[8,32,512]{2,1,0:T(8,128)} %param.13, s32[]{:T(128)S(6)} %select_n.54, s32[]{:T(128)S(6)} %select_n.53), kind=kLoop, calls=%fused_computation.20 | loop fusion | bytes 1048584 | tf_op jit(solution)/shard_map/dynamic_slice | solution.py:368
  10.9 0.7 fusion.8
  11.7 0.8 maximum_select_fusion.4
  12.5 1.2 copy.28
  13.9 15.1 %collective-permute-done.below_ref = f32[8,32,512]{2,1,0:T(8,128)S(1)} collective-permute-done((f32[8,32,512]{2,1,0:T(8,128)}, f32[8,32,512]{2,1,0:T(8,128)S(1)}, u32[]{:S(2)}, u32[]{:S(2)}) %collective-permute-start) | collective-permute-done | bytes 524320 | tf_op jit(solution)/shard_map/ppermute | solution.py:336
  29.0 0.5 collective-permute-start.4
  29.8 2.3 %copy.29 = f32[27,32,64]{1,2,0:T(8,128)} copy(f32[27,32,64]{2,1,0:T(8,128)} %collective-permute-done.6) | data formatting | bytes 442368 | tf_op jit(solution)/shard_map/ppermute | solution.py:340
  32.0 1.8 %fusion.2 = (f32[27,64,32]{1,2,0:T(8,128)S(1)}, f32[27,64,32]{1,2,0:T(8,128)S(1)}) fusion(f32[27,32,64]{1,2,0:T(8,128)} %copy.28, f32[27,32,64]{1,2,0:T(8,128)} %copy.29), kind=kLoop, calls=%fused_computation.10 | loop fusion | flops 110592 | bytes 884736 | tf_op jit(solution)/shard_map/concatenate | solution.py:370
  34.0 1.2 maximum_select_fusion
  35.3 1.4 copy.38.w_ref
  36.7 2.0 %fusion = f32[4,27,16,64]{3,2,0,1:T(8,128)S(1)} fusion(f32[27,32,4,16]{1,3,2,0:T(8,128)} %bitcast.18, f32[27,32,4,16]{1,3,2,0:T(8,128)} %bitcast.17, f32[27,64,2,16]{1,3,2,0:T(8,128)} %bitcast.20, f32[27,64,2,16]{1,3,2,0:T(8,128)} %bitcast.19, pred[]{:T(512)S(6)} %eq.3), kind=kLoop, calls=%fused_computation.2 | loop fusion | flops 331776 | bytes 1327105 | tf_op jit(solution)/shard_map/transpose | solution.py:314
  38.8 0.9 copy-done.1
  39.7 41.9 %level_forward.1 = (f32[4,32,512]{2,1,0:T(8,128)S(1)}, f32[4,32,512]{2,1,0:T(8,128)S(1)}, bf16[4,192,512]{2,1,0:T(8,128)(2,1)S(1)}, f32[27,32,64]{2,1,0:T(8,128)S(1)}, f32[27,32,64]{2,1,0:T(8,128)S(1)}) custom-call(s32[4,27]{1,0:T(4,128)S(1)} %constant_dynamic-slice_fusion.2.nb_ref, f32[4]{0:T(128)S(1)} %compare_convert_fusion.live_ref, ...), custom_call_target="tpu_custom_call" | custom-call | flops 35000000512 | bytes 105000000 | tf_op jit(solution)/shard_map/level_forward/pallas_call | solution.py:287
  81.6 24.0 %level_backward.1 = (f32[24,32,512]{2,1,0:T(8,128)S(1)}, f32[24,32,512]{2,1,0:T(8,128)S(1)}) custom-call(s32[4,27]{1,0:T(4,128)S(1)} %constant_dynamic-slice_fusion.2.nb_ref, bf16[4,192,512]{2,1,0:T(8,128)(2,1)S(1)} %get-tuple-element.12.grad_ref, f32[1728,64]{1,0:T(8,128)S(1)} %bitcast.15), custom_call_target="tpu_custom_call" | custom-call | flops 30000001024 | bytes 90000000 | tf_op jit(solution)/shard_map/level_backward/pallas_call | solution.py:316
  106.1 0.6 collective-permute-start.12
  106.8 2.9 %collective-permute-done.12 = f32[27,32,64]{2,1,0:T(8,128)S(1)} collective-permute-done((f32[27,32,64]{2,1,0:T(8,128)S(1)}, f32[27,32,64]{2,1,0:T(8,128)S(1)}, u32[]{:S(2)}, u32[]{:S(2)}) %collective-permute-start.12) | collective-permute-done | bytes 221216 | tf_op jit(solution)/shard_map/ppermute | solution.py:340
  109.9 2.4 %collective-permute-start.13 = (f32[27,32,64]{2,1,0:T(8,128)S(1)}, f32[27,32,64]{2,1,0:T(8,128)S(1)}, u32[]{:S(2)}, u32[]{:S(2)}) collective-permute-start(f32[27,32,64]{2,1,0:T(8,128)S(1)} %fusion.4), channel_id=1, source_target_pairs={{0,2},{2,0},{4,6},{6,4},{8,10},{10,8},{12,14},{14,12},{1,3},{3,1},... | collective-permute-start | bytes 663560 | tf_op jit(solution)/shard_map/ppermute | solution.py:349
  112.3 10.5 %collective-permute-done.13 = f32[27,32,64]{2,1,0:T(8,128)S(1)} collective-permute-done((f32[27,32,64]{2,1,0:T(8,128)S(1)}, f32[27,32,64]{2,1,0:T(8,128)S(1)}, u32[]{:S(2)}, u32[]{:S(2)}) %collective-permute-start.13) | collective-permute-done | bytes 221216 | tf_op jit(solution)/shard_map/ppermute | solution.py:349
  122.8 2.6 %collective-permute-start.14 = (f32[27,32,64]{2,1,0:T(8,128)S(1)}, f32[27,32,64]{2,1,0:T(8,128)S(1)}, u32[]{:S(2)}, u32[]{:S(2)}) collective-permute-start(f32[27,32,64]{2,1,0:T(8,128)S(1)} %add.43), channel_id=1, source_target_pairs={{0,4},{2,6},{4,0},{6,2},{8,12},{10,14},{12,8},{14,10},{1,5},{3,7},... | collective-permute-start | bytes 663560 | tf_op jit(solution)/shard_map/ppermute | solution.py:349
  125.9 1.3 collective-permute-start.10
  127.2 4.6 %collective-permute-start.11 = (f32[8,32,512]{2,1,0:T(8,128)S(1)}, f32[8,32,512]{2,1,0:T(8,128)S(1)}, u32[]{:S(2)}, u32[]{:S(2)}) collective-permute-start(f32[8,32,512]{2,1,0:T(8,128)S(1)} %get-tuple-element.20), channel_id=1, source_target_pairs={{0,2},{2,4},{4,6},{6,8},{8,10},{10,12},{12,14},{1,3},{3,5},{5,7},{... | collective-permute-start | bytes 1572872 | tf_op jit(solution)/shard_map/ppermute | solution.py:336
  131.8 4.7 %collective-permute-done.14 = f32[27,32,64]{2,1,0:T(8,128)S(1)} collective-permute-done((f32[27,32,64]{2,1,0:T(8,128)S(1)}, f32[27,32,64]{2,1,0:T(8,128)S(1)}, u32[]{:S(2)}, u32[]{:S(2)}) %collective-permute-start.14) | collective-permute-done | bytes 221216 | tf_op jit(solution)/shard_map/ppermute | solution.py:349
  136.6 3.1 %collective-permute-start.15 = (f32[27,32,64]{2,1,0:T(8,128)S(1)}, f32[27,32,64]{2,1,0:T(8,128)S(1)}, u32[]{:S(2)}, u32[]{:S(2)}) collective-permute-start(f32[27,32,64]{2,1,0:T(8,128)S(1)} %add.44), channel_id=1, source_target_pairs={{0,8},{2,10},{4,12},{6,14},{8,0},{10,2},{12,4},{14,6},{1,9},{3,11}... | collective-permute-start | bytes 663560 | tf_op jit(solution)/shard_map/ppermute | solution.py:349
  139.7 0.8 pad_maximum_fusion
  140.5 20.2 %collective-permute-done.15 = f32[27,32,64]{2,1,0:T(8,128)S(1)} collective-permute-done((f32[27,32,64]{2,1,0:T(8,128)S(1)}, f32[27,32,64]{2,1,0:T(8,128)S(1)}, u32[]{:S(2)}, u32[]{:S(2)}) %collective-permute-start.15) | collective-permute-done | bytes 221216 | tf_op jit(solution)/shard_map/ppermute | solution.py:349
  160.8 0.8 add.45
  161.6 1.0 fusion.1
  (45 shorter events, 2.2 us)
Async XLA Ops:
  0.6 8.5 %copy-start = (s32[8,27]{1,0:T(8,128)S(1)}, s32[8,27]{1,0:T(8,128)}, u32[]{:S(2)}) copy-start(s32[8,27]{1,0:T(8,128)} %param.9) | copy-start | bytes 2596
  0.6 11.8 %copy-start.6 = (f32[27,32,64]{2,1,0:T(8,128)S(1)}, f32[27,32,64]{2,1,0:T(8,128)}, u32[]{:S(2)}) copy-start(f32[27,32,64]{2,1,0:T(8,128)} %param.10) | copy-start | bytes 663556
  0.7 38.1 %collective-permute-start.2 = (f32[8,32,512]{2,1,0:T(8,128)}, f32[8,32,512]{2,1,0:T(8,128)S(1)}, u32[]{:S(2)}, u32[]{:S(2)}) collective-permute-start(f32[8,32,512]{2,1,0:T(8,128)} %own_ref.1), channel_id=1, source_target_pairs={{0,1},{1,0},{2,3},{3,2},{4,5},{5,4},{6,7},{7,6},{8,9},{9,8},{10,11... | collective-permute-start | bytes 1572872 | tf_op jit(solution)/shard_map/ppermute | solution.py:340
  1.2 27.8 %collective-permute-start = (f32[8,32,512]{2,1,0:T(8,128)}, f32[8,32,512]{2,1,0:T(8,128)S(1)}, u32[]{:S(2)}, u32[]{:S(2)}) collective-permute-start(f32[8,32,512]{2,1,0:T(8,128)} %own_ref.1), channel_id=1, source_target_pairs={{0,2},{2,4},{4,6},{6,8},{8,10},{10,12},{12,14},{1,3},{3,5},{5,7},{... | collective-permute-start | bytes 1572872 | tf_op jit(solution)/shard_map/ppermute | solution.py:336
  5.8 23.2 %collective-permute-start.3 = (f32[8,32,512]{2,1,0:T(8,128)}, f32[8,32,512]{2,1,0:T(8,128)S(1)}, u32[]{:S(2)}, u32[]{:S(2)}) collective-permute-start(f32[8,32,512]{2,1,0:T(8,128)} %own_ref.1), channel_id=1, source_target_pairs={{2,0},{4,2},{6,4},{8,6},{10,8},{12,10},{14,12},{3,1},{5,3},{7,5},{... | collective-permute-start | bytes 1572872 | tf_op jit(solution)/shard_map/ppermute | solution.py:336
  7.9 5.9 %collective-permute-start.7 = (f32[32,128]{0,1:T(8,128)S(1)}, f32[32,128]{0,1:T(8,128)S(1)}, u32[]{:S(2)}, u32[]{:S(2)}) collective-permute-start(f32[32,128]{0,1:T(8,128)S(1)} %copy.32), channel_id=1, source_target_pairs={{0,1},{1,0},{2,3},{3,2},{4,5},{5,4},{6,7},{7,6},{8,9},{9,8},{10,11... | collective-permute-start | bytes 49160 | tf_op jit(solution)/shard_map/ppermute | solution.py:340
  8.0 21.7 %collective-permute-start.6 = (f32[27,32,64]{2,1,0:T(8,128)}, f32[27,32,64]{2,1,0:T(8,128)}, u32[]{:S(2)}, u32[]{:S(2)}) collective-permute-start(f32[27,32,64]{2,1,0:T(8,128)} %param.10), channel_id=1, source_target_pairs={{0,1},{1,0},{2,3},{3,2},{4,5},{5,4},{6,7},{7,6},{8,9},{9,8},{10,11... | collective-permute-start | bytes 663560 | tf_op jit(solution)/shard_map/ppermute | solution.py:340
  13.8 25.0 %collective-permute-start.5 = (f32[4,32,512]{2,1,0:T(8,128)}, f32[4,32,512]{2,1,0:T(8,128)}, u32[]{:S(2)}, u32[]{:S(2)}) collective-permute-start(f32[4,32,512]{2,1,0:T(8,128)} %get-tuple-element.23), channel_id=1, source_target_pairs={{0,1},{1,0},{2,3},{3,2},{4,5},{5,4},{6,7},{7,6},{8,9},{9,8},{10,11... | collective-permute-start | bytes 786440 | tf_op jit(solution)/shard_map/ppermute | solution.py:340
  29.0 9.8 %collective-permute-start.1 = (f32[8,32,512]{2,1,0:T(8,128)S(1)}, f32[8,32,512]{2,1,0:T(8,128)S(1)}, u32[]{:S(2)}, u32[]{:S(2)}) collective-permute-start(f32[8,32,512]{2,1,0:T(8,128)S(1)} %collective-permute-done.below_ref), channel_id=1, source_target_pairs={{0,1},{1,0},{2,3},{3,2},{4,5},{5,4},{6,7},{7,6},{8,9},{9,8},{10,11... | collective-permute-start | bytes 1572872 | tf_op jit(solution)/shard_map/ppermute | solution.py:340
  29.0 9.8 %collective-permute-start.4 = (f32[8,32,512]{2,1,0:T(8,128)S(1)}, f32[8,32,512]{2,1,0:T(8,128)S(1)}, u32[]{:S(2)}, u32[]{:S(2)}) collective-permute-start(f32[8,32,512]{2,1,0:T(8,128)S(1)} %collective-permute-done.3.above_ref), channel_id=1, source_target_pairs={{0,1},{1,0},{2,3},{3,2},{4,5},{5,4},{6,7},{7,6},{8,9},{9,8},{10,11... | collective-permute-start | bytes 1572872 | tf_op jit(solution)/shard_map/ppermute | solution.py:340
  32.0 1.9 %copy-start.2 = (f32[27,32,64]{1,2,0:T(8,128)S(1)}, f32[27,32,64]{1,2,0:T(8,128)}, u32[]{:S(2)}) copy-start(f32[27,32,64]{1,2,0:T(8,128)} %copy.28) | copy-start | bytes 663556
  32.0 2.0 %copy-start.3 = (f32[27,32,64]{1,2,0:T(8,128)S(1)}, f32[27,32,64]{1,2,0:T(8,128)}, u32[]{:S(2)}) copy-start(f32[27,32,64]{1,2,0:T(8,128)} %copy.29) | copy-start | bytes 663556
  33.9 1.4 copy-start.4
  33.9 1.3 copy-start.5
  38.7 1.0 copy-start.1
  105.6 19.9 %collective-permute-start.9 = (f32[24,32,512]{2,1,0:T(8,128)S(1)}, f32[24,32,512]{2,1,0:T(8,128)S(1)}, u32[]{:S(2)}, u32[]{:S(2)}) collective-permute-start(f32[24,32,512]{2,1,0:T(8,128)S(1)} %get-tuple-element.14), channel_id=1, source_target_pairs={{0,1},{1,0},{2,3},{3,2},{4,5},{5,4},{6,7},{7,6},{8,9},{9,8},{10,11... | collective-permute-start | bytes 4718600 | tf_op jit(solution)/shard_map/ppermute | solution.py:340
  106.1 3.6 %collective-permute-start.12 = (f32[27,32,64]{2,1,0:T(8,128)S(1)}, f32[27,32,64]{2,1,0:T(8,128)S(1)}, u32[]{:S(2)}, u32[]{:S(2)}) collective-permute-start(f32[27,32,64]{2,1,0:T(8,128)S(1)} %maximum_select_fusion.3), channel_id=1, source_target_pairs={{0,1},{1,0},{2,3},{3,2},{4,5},{5,4},{6,7},{7,6},{8,9},{9,8},{10,11... | collective-permute-start | bytes 663560 | tf_op jit(solution)/shard_map/ppermute | solution.py:340
  109.9 12.9 %collective-permute-start.13 = (f32[27,32,64]{2,1,0:T(8,128)S(1)}, f32[27,32,64]{2,1,0:T(8,128)S(1)}, u32[]{:S(2)}, u32[]{:S(2)}) collective-permute-start(f32[27,32,64]{2,1,0:T(8,128)S(1)} %fusion.4), channel_id=1, source_target_pairs={{0,2},{2,0},{4,6},{6,4},{8,10},{10,8},{12,14},{14,12},{1,3},{3,1},... | collective-permute-start | bytes 663560 | tf_op jit(solution)/shard_map/ppermute | solution.py:349
  112.3 27.4 %collective-permute-start.8 = (f32[4,32,512]{2,1,0:T(8,128)S(1)}, f32[4,32,512]{2,1,0:T(8,128)S(1)}, u32[]{:S(2)}, u32[]{:S(2)}) collective-permute-start(f32[4,32,512]{2,1,0:T(8,128)S(1)} %get-tuple-element.11), channel_id=1, source_target_pairs={{0,1},{1,0},{2,3},{3,2},{4,5},{5,4},{6,7},{7,6},{8,9},{9,8},{10,11... | collective-permute-start | bytes 786440 | tf_op jit(solution)/shard_map/ppermute | solution.py:340
  122.8 13.7 %collective-permute-start.14 = (f32[27,32,64]{2,1,0:T(8,128)S(1)}, f32[27,32,64]{2,1,0:T(8,128)S(1)}, u32[]{:S(2)}, u32[]{:S(2)}) collective-permute-start(f32[27,32,64]{2,1,0:T(8,128)S(1)} %add.43), channel_id=1, source_target_pairs={{0,4},{2,6},{4,0},{6,2},{8,12},{10,14},{12,8},{14,10},{1,5},{3,7},... | collective-permute-start | bytes 663560 | tf_op jit(solution)/shard_map/ppermute | solution.py:349
  125.9 35.7 %collective-permute-start.10 = (f32[8,32,512]{2,1,0:T(8,128)S(1)}, f32[8,32,512]{2,1,0:T(8,128)S(1)}, u32[]{:S(2)}, u32[]{:S(2)}) collective-permute-start(f32[8,32,512]{2,1,0:T(8,128)S(1)} %get-tuple-element.19), channel_id=1, source_target_pairs={{2,0},{4,2},{6,4},{8,6},{10,8},{12,10},{14,12},{3,1},{5,3},{7,5},{... | collective-permute-start | bytes 1572872 | tf_op jit(solution)/shard_map/ppermute | solution.py:336
  127.2 34.4 %collective-permute-start.11 = (f32[8,32,512]{2,1,0:T(8,128)S(1)}, f32[8,32,512]{2,1,0:T(8,128)S(1)}, u32[]{:S(2)}, u32[]{:S(2)}) collective-permute-start(f32[8,32,512]{2,1,0:T(8,128)S(1)} %get-tuple-element.20), channel_id=1, source_target_pairs={{0,2},{2,4},{4,6},{6,8},{8,10},{10,12},{12,14},{1,3},{3,5},{5,7},{... | collective-permute-start | bytes 1572872 | tf_op jit(solution)/shard_map/ppermute | solution.py:336
  136.6 24.2 %collective-permute-start.15 = (f32[27,32,64]{2,1,0:T(8,128)S(1)}, f32[27,32,64]{2,1,0:T(8,128)S(1)}, u32[]{:S(2)}, u32[]{:S(2)}) collective-permute-start(f32[27,32,64]{2,1,0:T(8,128)S(1)} %add.44), channel_id=1, source_target_pairs={{0,8},{2,10},{4,12},{6,14},{8,0},{10,2},{12,4},{14,6},{1,9},{3,11}... | collective-permute-start | bytes 663560 | tf_op jit(solution)/shard_map/ppermute | solution.py:349
